TPU v7x, 256 devices: a whole 4x4x8 slice. The times are simulated.
256 devices in a mesh: ens: 4 (over x_hi, core), space: 64 (over x_lo, z, y).
Axes of the slice: x: 4 (x_hi: 2, x_lo: 2; x = x_hi * 2 + x_lo), y: 4, z: 8, core: 2. Of those that a mesh axis runs over, the one named last changes fastest.
Arguments:
- checkpoints: bfloat16 [32, 2, 3, 2048, 2048], P('ens', None, None, 'space'), may hold values from -6 to 6
- section_index: int32 [32], P('ens'), may hold values from 0 to 1
- targets: bfloat16 [32, 2048, 2048], P('ens', 'space'), may hold values from -6 to 6
- sea_mask: int32 [2048, 2048], P('space'), may hold values 0 or 1
- basis_rows: bfloat16 [2048, 1024], P('space'), may hold values from -0.5 to 0.5
- basis_cols: bfloat16 [2048, 1024], replicated, may hold values from -0.1875 to 0.1875
- control: float32 [1024, 1024], P('space'), may hold values from -6 to 6
Outputs:
- control_next: float32 [1024, 1024], P('space')
Inputs may be any that keep to these rules, and one draw needn't show every extreme that they name: `section_index`: selects one of the 2 slots.
All inputs are finite; a program needn't handle non-finite values. No bound on the sum of `sea_mask` on one device may be relied on, other than what follows from the above.
Results may differ from a plain program's by a relative error of at most 0.0014.
The roundings to bfloat16 on the way count: a program that leaves them out, or rounds other values in their place, can miss the bound.
Values may be sent and summed in bfloat16 or wider, within the bound.
A program may use at most 128 MiB of HBM per device.

v0:
```python
import jax
import jax.numpy as jnp
from jax import lax
from jax.sharding import PartitionSpec as P

DEPTH = 1.0
GRAVITY = 1.0
CORIOLIS = 0.5
FRICTION = 0.1
TIME_STEP = 0.3
STEP_SIZE = 1.0
EPSILON = 1e-06


def with_halo(value, sides, width):
    for axis, dim in sides:
        count, length = (lax.axis_size(axis), value.shape[dim])
        up = [(i, (i + 1) % count) for i in range(count - 1)]
        down = [(j, i) for i, j in up]
        last = lax.slice_in_dim(value, length - width, length, axis=dim)
        initial = lax.slice_in_dim(value, 0, width, axis=dim)
        before = lax.ppermute(last, axis, up)
        after = lax.ppermute(initial, axis, down)
        value = jnp.concatenate([before, value, after], axis=dim)
    return value


def across_columns(field):
    widths = [(0, 0)] * (field.ndim - 1) + [(1, 1)]
    padded = jnp.pad(field, widths)
    return 0.5 * (padded[..., 2:] - padded[..., :-2])


def across_rows(extended):
    return 0.5 * (extended[..., 2:, :] - extended[..., :-2, :])


def state_edges(height, north):
    stacked = jnp.stack([height, north], axis=1)
    return with_halo(stacked, (("space", 2),), 1)


def height_change(height, east, edges):
    flux_ext = (DEPTH + edges[:, 0]) * edges[:, 1]
    return -(across_columns((DEPTH + height) * east) + across_rows(flux_ext))


def expand(coefficients, basis_cols):
    return lax.dot_general(
        coefficients, basis_cols, (((1,), (1,)), ((), ())), preferred_element_type=jnp.float32
    )


def normalized(gradient_rows, control_rows, width):
    total = lax.psum(jnp.sum(gradient_rows * gradient_rows), "space")
    return control_rows - STEP_SIZE * gradient_rows / jnp.sqrt(total / (width * width) + EPSILON)


def stencil_per_step(start, targets, sea, stress_x, stress_y):
    height_start, east_start, north_start = (start[:, 0], start[:, 1], start[:, 2])
    edges = state_edges(height_start, north_start)
    change_height = height_change(height_start, east_start, edges)
    change_east = (
        CORIOLIS * north_start
        - GRAVITY * across_columns(height_start)
        - FRICTION * east_start
        + stress_x
    )
    change_north = (
        -CORIOLIS * east_start
        - GRAVITY * across_rows(edges[:, 0])
        - FRICTION * north_start
        + stress_y
    )
    height_mid = sea * (height_start + TIME_STEP * change_height)
    east_mid = sea * (east_start + TIME_STEP * change_east)
    north_mid = sea * (north_start + TIME_STEP * change_north)
    edges_mid = state_edges(height_mid, north_mid)
    change_mid = height_change(height_mid, east_mid, edges_mid)
    height_end = sea * (0.5 * height_start + 0.5 * (height_mid + TIME_STEP * change_mid))
    adjoint_height = 0.5 * sea * (height_end - targets.astype(jnp.float32))
    adjoint_ext = with_halo(adjoint_height, (("space", 1),), 1)
    weight = TIME_STEP * TIME_STEP * sea * (DEPTH + height_mid)
    push_east = jnp.sum(weight * across_columns(adjoint_height), axis=0)
    push_north = jnp.sum(weight * across_rows(adjoint_ext), axis=0)
    east_edges = with_halo(push_east, (("space", 0),), 1)
    return across_rows(east_edges) - across_columns(push_north)


def on_device(checkpoints, section_index, targets, sea_mask, basis_rows, basis_cols, control):
    narrow = control.astype(jnp.bfloat16)
    reach = 1
    coeffs = jnp.dot(
        basis_rows,
        lax.all_gather(narrow, "space", axis=0, tiled=True),
        preferred_element_type=jnp.float32,
    ).astype(jnp.bfloat16)
    potential_ext = with_halo(expand(coeffs, basis_cols), (("space", 0),), reach)
    stress_x = -across_rows(potential_ext)
    stress_y = across_columns(potential_ext[1:-1])
    slots = checkpoints.shape[1]
    chosen = section_index[:, None, None, None, None] == lax.broadcasted_iota(
        jnp.int32, (1, slots, 1, 1, 1), 1
    )
    start = jnp.sum(
        jnp.where(chosen, checkpoints, jnp.zeros_like(checkpoints)), axis=1, dtype=jnp.float32
    )
    sea = sea_mask.astype(jnp.float32)
    local_grad = stencil_per_step(start, targets, sea, stress_x, stress_y)
    summed = lax.psum(local_grad, "ens")
    summed_narrow = summed.astype(jnp.bfloat16)
    width = control.shape[1]
    projected = jnp.dot(summed_narrow, basis_cols, preferred_element_type=jnp.float32).astype(
        jnp.bfloat16
    )
    gradient_rows = lax.psum_scatter(
        lax.dot_general(
            basis_rows, projected, (((0,), (0,)), ((), ())), preferred_element_type=jnp.float32
        ),
        "space",
        scatter_dimension=0,
        tiled=True,
    )
    return normalized(gradient_rows, control, width)


def solution(mesh):
    return jax.shard_map(
        on_device,
        mesh=mesh,
        in_specs=(
            P("ens", None, None, "space", None),
            P("ens"),
            P("ens", "space", None),
            P("space", None),
            P("space", None),
            P(),
            P("space", None),
        ),
        out_specs=P("space", None),
        check_vma=False,
    )
```

profile of v0, /device:TPU:2, one launch (start us, length us, event | category | flops | bytes accessed | tf_op | source)
XLA Modules:
  0.0 894.7 jit_solution(11829414807353290444)
XLA Ops:
  6.5 1.5 convert_element_type.31
  8.1 0.0 reduce-scatter.4.cloned.1.call-start
  8.1 0.7 iota_compare_fusion
  8.8 5.5 convert_reduce_fusion
  14.3 2.3 slice_bitcast_fusion.4
  16.6 0.2 pad_maximum_fusion.11
  16.8 3.5 collective-permute-start
  20.3 8.8 collective-permute-start.1
  29.1 1.6 add_multiply_fusion
  30.7 0.1 collective-permute-done
  30.8 1.5 collective-permute-done.1
  32.4 1.1 pad_maximum_fusion
  33.5 2.4 copy-done.2
  35.9 0.4 fusion.1
  36.3 274.4 %all-gather.2.cloned.1.call-done = bf16[1024,1024]{1,0:T(8,128)(2,1)} async-done(((bf16[16,1024]{1,0:T(8,128)(2,1)}), bf16[1024,1024]{1,0:T(8,128)(2,1)}) %all-gather.2.cloned.1.call-update) | async-done | bytes 2097168 | tf_op jit(solution)/shard_map/all_gather | solution.py:95
  310.7 4.5 fusion.44
  315.2 6.9 collective-permute-start.2
  322.2 2.2 collective-permute-start.3
  324.3 1.9 slice_bitcast_fusion.1
  326.3 5.9 collective-permute-done.3
  332.2 0.2 fusion.46
  332.4 5.2 fusion.17
  337.6 0.2 pad_maximum_fusion.9
  337.9 1.9 collective-permute-start.4
  339.8 8.1 collective-permute-start.5
  348.0 1.0 collective-permute-done.4
  348.9 1.5 collective-permute-done.5
  350.4 0.8 pad_maximum_fusion.1
  351.2 0.4 fusion
  351.6 0.8 copy-done.6
  352.4 2.9 fusion.27
  355.3 0.1 fusion.58
  355.4 8.6 collective-permute-start.8
  364.0 2.1 collective-permute-start.9
  366.1 8.3 collective-permute-done.9
  374.4 1.3 fusion.31
  375.7 1.9 collective-permute-start.6
  377.6 3.9 collective-permute-start.7
  381.6 5.8 collective-permute-done.7
  387.4 0.2 fusion.49
  387.6 16.2 %all-reduce.7 = bf16[32,2048]{1,0:T(8,128)(2,1)S(1)} all-reduce(f32[32,2048]{1,0:T(8,128)S(1)} %fusion.49), channel_id=1, replica_groups=mesh['ens'=4,'space'=64] {'ens'}, use_global_device_ids=true, to_apply=%region_3.4 | all-reduce | flops 65536 | bytes 393216 | tf_op jit(solution)/shard_map/psum | solution.py:110
  403.9 5.6 convolution_bitcast_fusion
  409.5 5.4 copy.17
  414.9 315.1 %reduce-scatter.4.cloned.1.call-done = f32[16,1024]{1,0:T(8,128)} async-done(((f32[1024,1024]{1,0:T(8,128)}), f32[16,1024]{1,0:T(8,128)}) %reduce-scatter.4.cloned.1.call-update) | async-done | bytes 65552 | tf_op jit(solution)/shard_map/reduce_scatter | solution.py:116
  730.0 1.0 copy.18
  731.0 0.7 multiply_reduce_fusion
  731.8 153.9 %psum.15 = f32[]{:T(128)} all-reduce(f32[]{:T(128)} %multiply_reduce_fusion), channel_id=1, replica_groups=mesh['ens'=4,'space'=64] {'space'}, use_global_device_ids=true, to_apply=%region_6.7 | all-reduce | flops 1 | bytes 8 | tf_op jit(solution)/shard_map/psum | solution.py:55
  886.4 1.5 divide_subtract_fusion
  (24 shorter events, 0.2 us)
Async XLA Ops:
  6.5 304.1 %copy-start = (bf16[32,1024]{1,0:T(8,128)(2,1)S(1)}, bf16[32,1024]{1,0:T(8,128)(2,1)}, u32[]{:S(2)}) copy-start(bf16[32,1024]{1,0:T(8,128)(2,1)} %param.11) | copy-start | bytes 196612
  6.5 304.1 %all-gather.2.cloned.1.call-start = ((), (), s32[]{:S(2)}) async-start(), calls=%async_computation.1 | async-start | bytes 2129920 | tf_op jit(solution)/shard_map/all_gather | solution.py:95
  8.1 722.0 %reduce-scatter.4.cloned.1.call-start = ((), (), s32[]{:S(2)}) async-start(), calls=%async_computation.2 | async-start | bytes 4259840 | tf_op jit(solution)/shard_map/reduce_scatter | solution.py:116
  14.3 14.7 %copy-start.1 = (f32[8,3,32,2048]{3,2,1,0:T(8,128)}, f32[8,3,32,2048]{3,2,1,0:T(8,128)S(1)}, u32[]{:S(2)}) copy-start(f32[8,3,32,2048]{3,2,1,0:T(8,128)S(1)} %convert_reduce_fusion) | copy-start | bytes 18874372
  16.8 14.0 %collective-permute-start = (f32[8,2,1,2048]{3,2,0,1:T(1,128)S(1)}, f32[8,2,1,2048]{3,2,0,1:T(1,128)S(1)}, u32[]{:S(2)}, u32[]{:S(2)}) collective-permute-start(f32[8,2,1,2048]{3,2,0,1:T(1,128)S(1)} %get-tuple-element.15), channel_id=1, source_target_pairs={{0,1},{1,2},{2,3},{3,4},{4,5},{5,6},{6,7},{7,8},{8,9},{9,10},{10,1... | collective-permute-start | bytes 393224 | tf_op jit(solution)/shard_map/ppermute | solution.py:22
  20.3 10.4 %copy-start.5 = (s32[32,2048]{1,0:T(8,128)S(1)}, s32[32,2048]{1,0:T(8,128)}, u32[]{:S(2)}) copy-start(s32[32,2048]{1,0:T(8,128)} %param.10) | copy-start | bytes 786436
  20.3 12.0 %collective-permute-start.1 = (f32[8,2,1,2048]{3,2,0,1:T(1,128)S(1)}, f32[8,2,1,2048]{3,2,0,1:T(1,128)S(1)}, u32[]{:S(2)}, u32[]{:S(2)}) collective-permute-start(f32[8,2,1,2048]{3,2,0,1:T(1,128)S(1)} %get-tuple-element.16), channel_id=1, source_target_pairs={{1,0},{2,1},{3,2},{4,3},{5,4},{6,5},{7,6},{8,7},{9,8},{10,9},{11,1... | collective-permute-start | bytes 393224 | tf_op jit(solution)/shard_map/ppermute | solution.py:23
  33.5 2.4 copy-start.2
  315.2 11.1 %collective-permute-start.2 = (f32[1,2048]{1,0:T(1,128)S(1)}, f32[1,2048]{1,0:T(1,128)S(1)}, u32[]{:S(2)}, u32[]{:S(2)}) collective-permute-start(f32[1,2048]{1,0:T(1,128)S(1)} %get-tuple-element.25), channel_id=1, source_target_pairs={{1,0},{2,1},{3,2},{4,3},{5,4},{6,5},{7,6},{8,7},{9,8},{10,9},{11,1... | collective-permute-start | bytes 24584 | tf_op jit(solution)/shard_map/ppermute | solution.py:23
  322.1 10.3 %copy-start.3 = (f32[8,32,2048]{2,1,0:T(8,128)S(1)}, f32[8,32,2048]{2,1,0:T(8,128)}, u32[]{:S(2)}) copy-start(f32[8,32,2048]{2,1,0:T(8,128)} %get-tuple-element.11) | copy-start | bytes 6291460
  322.1 10.3 %copy-start.4 = (f32[8,32,2048]{2,1,0:T(8,128)S(1)}, f32[8,32,2048]{2,1,0:T(8,128)}, u32[]{:S(2)}) copy-start(f32[8,32,2048]{2,1,0:T(8,128)} %add_multiply_fusion) | copy-start | bytes 6291460
  322.2 10.0 %collective-permute-start.3 = (f32[1,2048]{1,0:T(1,128)S(1)}, f32[1,2048]{1,0:T(1,128)S(1)}, u32[]{:S(2)}, u32[]{:S(2)}) collective-permute-start(f32[1,2048]{1,0:T(1,128)S(1)} %get-tuple-element.26), channel_id=1, source_target_pairs={{0,1},{1,2},{2,3},{3,4},{4,5},{5,6},{6,7},{7,8},{8,9},{9,10},{10,1... | collective-permute-start | bytes 24584 | tf_op jit(solution)/shard_map/ppermute | solution.py:22
  337.9 11.1 %collective-permute-start.4 = (f32[8,2,1,2048]{3,2,0,1:T(1,128)S(1)}, f32[8,2,1,2048]{3,2,0,1:T(1,128)S(1)}, u32[]{:S(2)}, u32[]{:S(2)}) collective-permute-start(f32[8,2,1,2048]{3,2,0,1:T(1,128)S(1)} %get-tuple-element.13), channel_id=1, source_target_pairs={{0,1},{1,2},{2,3},{3,4},{4,5},{5,6},{6,7},{7,8},{8,9},{9,10},{10,1... | collective-permute-start | bytes 393224 | tf_op jit(solution)/shard_map/ppermute | solution.py:22
  339.8 10.6 %collective-permute-start.5 = (f32[8,2,1,2048]{3,2,0,1:T(1,128)S(1)}, f32[8,2,1,2048]{3,2,0,1:T(1,128)S(1)}, u32[]{:S(2)}, u32[]{:S(2)}) collective-permute-start(f32[8,2,1,2048]{3,2,0,1:T(1,128)S(1)} %get-tuple-element.14), channel_id=1, source_target_pairs={{1,0},{2,1},{3,2},{4,3},{5,4},{6,5},{7,6},{8,7},{9,8},{10,9},{11,1... | collective-permute-start | bytes 393224 | tf_op jit(solution)/shard_map/ppermute | solution.py:23
  351.2 1.2 copy-start.6
  355.4 10.7 %collective-permute-start.8 = (f32[8,1,2048]{2,1,0:T(1,128)S(1)}, f32[8,1,2048]{2,1,0:T(1,128)S(1)}, u32[]{:S(2)}, u32[]{:S(2)}) collective-permute-start(f32[8,1,2048]{2,1,0:T(1,128)S(1)} %get-tuple-element.17), channel_id=1, source_target_pairs={{1,0},{2,1},{3,2},{4,3},{5,4},{6,5},{7,6},{8,7},{9,8},{10,9},{11,1... | collective-permute-start | bytes 196616 | tf_op jit(solution)/shard_map/ppermute | solution.py:23
  364.0 10.4 %collective-permute-start.9 = (f32[8,1,2048]{2,1,0:T(1,128)S(1)}, f32[8,1,2048]{2,1,0:T(1,128)S(1)}, u32[]{:S(2)}, u32[]{:S(2)}) collective-permute-start(f32[8,1,2048]{2,1,0:T(1,128)S(1)} %get-tuple-element.18), channel_id=1, source_target_pairs={{0,1},{1,2},{2,3},{3,4},{4,5},{5,6},{6,7},{7,8},{8,9},{9,10},{10,1... | collective-permute-start | bytes 196616 | tf_op jit(solution)/shard_map/ppermute | solution.py:22
  375.7 5.9 collective-permute-start.6
  377.6 9.8 %collective-permute-start.7 = (f32[1,2048]{1,0:T(1,128)S(1)}, f32[1,2048]{1,0:T(1,128)S(1)}, u32[]{:S(2)}, u32[]{:S(2)}) collective-permute-start(f32[1,2048]{1,0:T(1,128)S(1)} %get-tuple-element.20), channel_id=1, source_target_pairs={{0,1},{1,2},{2,3},{3,4},{4,5},{5,6},{6,7},{7,8},{8,9},{9,10},{10,1... | collective-permute-start | bytes 24584 | tf_op jit(solution)/shard_map/ppermute | solution.py:22
  414.8 471.5 %copy-start.7 = (f32[16,1024]{1,0:T(8,128)S(1)}, f32[16,1024]{1,0:T(8,128)}, u32[]{:S(2)}) copy-start(f32[16,1024]{1,0:T(8,128)} %param.13) | copy-start | bytes 196612
Sparse Core Ops, SparseCore 0:
  9.1 301.4 all-gather.1
  415.0 314.9 reduce-scatter.3
where the time goes:
time: 897 us; the launch traced here: 895 us
  waiting for transfers between devices  614 us (68%)
  blocking collectives  170 us (19%)
  starting transfers between devices  48 us (5%)
  other arithmetic  24.5 us (3%)
  between operations  14.4 us (2%)
  local copies, waits for them, and re-layouts  13.9 us (2%)
  matrix products  10.1 us (1%)
    reduce_scatter x1, waiting for transfers between devices, on_device(): lax.psum_scatter(lax.dot_general(basis_rows, projected, (((0,), (0,)), ((...  315 us
    all_gather x1, waiting for transfers between devices, on_device(): lax.all_gather(narrow, 'space', axis=0, tiled=True)  274 us
    psum x1, blocking collectives, normalized(): total = lax.psum(jnp.sum(gradient_rows * gradient_rows), 'space')  154 us
    ppermute x5, starting transfers between devices, with_halo(): after = lax.ppermute(initial, axis, down)  34.3 us
    ppermute x5, waiting for transfers between devices, with_halo(): before = lax.ppermute(last, axis, up)  21.1 us
  transfers between devices with their start and end apart: 12, of which 9 were waited for; matrix products, arithmetic and copies ran while one was open for 2% of the time, Pallas kernels for 0%

commit v1 on v0

v1 whole, which is shorter than its diff:
```python
import functools

import jax
import jax.numpy as jnp
from jax import lax
from jax.experimental import pallas as pl
from jax.experimental.pallas import tpu as pltpu
from jax.sharding import PartitionSpec as P

MESH = pl.DeviceIdType.MESH
F32 = jnp.float32
BF16 = jnp.bfloat16
EPSILON = 1e-06
LANES = 128
LINE = 8
ENS = 4
YN = 4


def kernel(
    zn,
    si_ref, ck_hbm, tg_hbm, mask_hbm, br_hbm, bc_hbm, ct_hbm, out_ref,
    ck, tg, mk_in, br, bc, ct,
    ctl_s, ctl_g, ext, bhal, hs, hr, hal, mk,
    hm_s, fx_s, fy_s, ab_s, cfs, cfg, pot, px, py, gx, gy,
    gs, gr, ps, pr, g_s, gyr, gy_s, gzr, fs, fr, sys_, syr, szs, szr,
    load_sem, send_sem, recv_sem,
):
    states, rows, cols = ck.shape[0], ck.shape[3], ck.shape[4]
    ring = rows + 8
    nk = cols // LANES
    basis = br.shape[1]
    piece = cols // ENS
    e = lax.axis_index("ens")
    t = lax.axis_index("space")
    x = t // (zn * YN)
    z = (t // YN) % zn
    y = t % YN
    j = x * ENS + e
    count = 2 * zn * YN

    def dev(e2, x2, z2, y2):
        return (e2, (x2 * zn + z2) * YN + y2)

    line = []
    for d in range(1, LINE):
        j2 = (j + d) % LINE
        line.append((j2, dev(j2 % ENS, j2 // ENS, z, y)))
    ys = []
    for d in range(1, YN):
        y2 = (y + d) % YN
        ys.append((y2, dev(e, x, z, y2)))
    zs = []
    for d in range(1, zn):
        z2 = (z + d) % zn
        zs.append((z2, dev(e, x, z2, y)))
    es = []
    for d in range(1, ENS):
        e2 = (e + d) % ENS
        es.append((e2, (e2, t)))
    partner = dev(e, 1 - x, z, y)
    after = (e, (t + 1) % count)
    before = (e, (t + count - 1) % count)

    base = [0]

    def sems(n):
        at = base[0]
        base[0] += n
        return at

    loads = [
        pltpu.make_async_copy(src, dst, load_sem.at[i])
        for i, (src, dst) in enumerate(
            ((ct_hbm, ct), (br_hbm, br), (ck_hbm, ck), (tg_hbm, tg), (mask_hbm, mk_in), (bc_hbm, bc))
        )
    ]
    for load in loads:
        load.start()

    barrier = pltpu.get_barrier_semaphore()
    greet = [d for _, d in line] + [d for _, d in ys] + [d for _, d in zs] + [after, before]
    for d in greet:
        pl.semaphore_signal(barrier, inc=1, device_id=d, device_id_type=MESH)

    def copy(src, dst, at_send, at_recv, device):
        return pltpu.make_async_remote_copy(
            src_ref=src,
            dst_ref=dst,
            send_sem=send_sem.at[at_send],
            recv_sem=recv_sem.at[at_recv],
            device_id=device,
            device_id_type=MESH,
        )

    sent = []

    def exchange(peers, me, n, src_of, dst_of):
        at = sems(n)
        for i, (p, device) in enumerate(peers):
            c = copy(src_of(p), dst_of(me), at + i, at + me, device)
            c.start()
            sent.append(c)

        def wait():
            for p, device in peers:
                copy(src_of(p), dst_of(p), at, at + p, device).wait_recv()

        return wait

    def single(src, dst, device):
        at = sems(1)
        c = copy(src, dst, at, at, device)
        c.start()
        sent.append(c)
        return c.wait_recv

    loads[0].wait()
    for b in range(LINE):
        ctl_s[b] = ct[:, b * LANES : (b + 1) * LANES].astype(BF16)
    ctl_g[x, z, y] = ctl_s[j]
    pl.semaphore_wait(barrier, len(greet))
    a0 = single(ctl_s.at[(1 - x) * ENS + e], ctl_g.at[x, z, y], partner)
    loads[1].wait()
    top_rows = single(br.at[0:16], bhal.at[0], before)
    end_rows = single(br.at[rows - 16 : rows], bhal.at[1], after)
    a0()
    ay = exchange(ys, y, YN, lambda p: ctl_g.at[:, z, y], lambda p: ctl_g.at[:, z, p])

    loads[2].wait()
    loads[3].wait()
    loads[4].wait()
    sub = lax.broadcasted_iota(jnp.int32, (8, cols), 0)

    def tiles(s, field, first):
        slot = si_ref[s]
        block = ck[s, slot, field, first : first + 16, :].astype(F32)
        return block[0:8] if first == 0 else block[8:16]

    last = rows - 16
    for half in range(states // 2):
        up, down = [], []
        for s in (2 * half, 2 * half + 1):
            h, u, v = (tiles(s, f, 0) for f in range(3))
            up.append(jnp.where(sub < 3, h, jnp.where(sub < 6, pltpu.roll(v, 3, 0), pltpu.roll(u, 6, 0))))
            h, u, v = (tiles(s, f, last) for f in range(3))
            down.append(jnp.where(sub >= 5, h, jnp.where(sub >= 2, pltpu.roll(v, 5, 0), pltpu.roll(u, 2, 0))))
        hs[0, half] = jnp.concatenate(up, axis=0).astype(BF16)
        hs[1, half] = jnp.concatenate(down, axis=0).astype(BF16)
    up = jnp.zeros((8, cols), F32)
    down = jnp.zeros((8, cols), F32)
    for s in range(states):
        first = tg[s, 0:16, :].astype(F32)[0:8]
        up = jnp.where(sub == s, first if s == 0 else pltpu.roll(first, s, 0), up)
        final = tg[s, last : last + 16, :].astype(F32)[8:16]
        down = jnp.where(sub == s, final if s == 7 else pltpu.roll(final, s + 1, 0), down)
    hs[0, states // 2] = jnp.concatenate([up, mk_in[0:8, :].astype(F32)], axis=0).astype(BF16)
    hs[1, states // 2] = jnp.concatenate([down, mk_in[rows - 8 : rows, :].astype(F32)], axis=0).astype(BF16)
    from_after = single(hs.at[0], hr.at[0], before)
    from_before = single(hs.at[1], hr.at[1], after)

    ay()
    az = exchange(zs, z, zn, lambda p: ctl_g.at[:, z], lambda p: ctl_g.at[:, p])

    low_end = jnp.where(t < count - 1, 4, 0)
    high_start = jnp.where(t > 0, 4, 8)

    top_rows()
    end_rows()
    subb = lax.broadcasted_iota(jnp.int32, (8, basis), 0)
    edge = jnp.where(
        subb < low_end,
        bhal[0].astype(F32)[0:8],
        jnp.where(subb >= high_start, bhal[1].astype(F32)[8:16], 0.0),
    )
    ext[x, 0:rows] = br[...]
    ext[x, rows : rows + 16] = jnp.concatenate([edge, jnp.zeros_like(edge)], axis=0).astype(BF16)
    other_ext = single(ext.at[x], ext.at[x], partner)

    from_after()
    from_before()

    def joined(low, high):
        return jnp.where(sub < low_end, low, jnp.where(sub >= high_start, high, 0.0))

    for half in range(states // 2):
        low2 = hr[0, half].astype(F32)
        high2 = hr[1, half].astype(F32)
        for i in range(2):
            s = 2 * half + i
            low, high = low2[8 * i : 8 * i + 8], high2[8 * i : 8 * i + 8]
            hal[s, 0] = joined(low, high)
            hal[s, 1] = joined(pltpu.roll(low, 2, 0), pltpu.roll(high, 6, 0))
            hal[s, 2] = joined(pltpu.roll(low, 5, 0), pltpu.roll(high, 3, 0))
    low2 = hr[0, states // 2].astype(F32)
    high2 = hr[1, states // 2].astype(F32)
    for s in range(states):
        low, high = low2[0:8], high2[0:8]
        low = low if s == 0 else pltpu.roll(low, 8 - s, 0)
        high = high if s == 7 else pltpu.roll(high, 7 - s, 0)
        hal[s, 3] = joined(low, high)
    mk[0:rows] = mk_in[...].astype(F32)
    mk[rows:ring] = joined(low2[8:16], high2[8:16])

    az()
    other_ext()
    control_all = ctl_g[...].reshape(basis, LANES)
    lhs = ext[...].reshape(2 * (rows + 16), basis)
    cf = jnp.dot(lhs, control_all, preferred_element_type=F32).astype(BF16)
    cfs[...] = cf.reshape(2, rows + 16, LANES)
    cfg[j] = cfs[x]
    wait_cf = exchange(line, j, LINE, lambda p: cfs.at[p // ENS], lambda p: cfg.at[p])

    lane = lax.broadcasted_iota(jnp.int32, (ring, LANES), 1)
    is_first = lane == 0
    is_last = lane == LANES - 1

    def row_diff(q):
        return pltpu.roll(q, ring - 1, 0) - pltpu.roll(q, 1, 0)

    def turned(q):
        return pltpu.roll(q, LANES - 1, 1), pltpu.roll(q, 1, 1)

    def column_diff(turns, k):
        left = turns[k - 1][1] if k > 0 else 0.0
        right = turns[k + 1][0] if k < nk - 1 else 0.0
        return jnp.where(is_last, right, turns[k][0]) - jnp.where(is_first, left, turns[k][1])

    def at(k):
        return slice(k * LANES, (k + 1) * LANES)

    def before_stress(s, carry):
        slot = si_ref[s]

        def full(field, k):
            own = ck[s, slot, field, :, at(k)].astype(F32)
            return jnp.concatenate([own, hal[s, field, :, at(k)]], axis=0)

        kept, fxt, ht = {}, {}, {}
        for step in range(nk + 1):
            if step < nk:
                k = step
                h, u, v = (full(f, k) for f in range(3))
                g = 1.0 + h
                fx, fy = g * u, g * v
                kept[k] = (h, u, v, row_diff(fy), row_diff(h))
                fxt[k], ht[k] = turned(fx), turned(h)
            if step >= 1:
                k = step - 1
                h, u, v, dyf, dyh = kept.pop(k)
                w = 0.15 * (column_diff(fxt, k) + dyf)
                hm = mk[:, at(k)] * ((1.0 + h) - w)
                ub = 0.97 * u + 0.15 * (v - column_diff(ht, k))
                vb = 0.97 * v - 0.15 * (u + dyh)
                seen = jnp.concatenate([tg[s, :, at(k)].astype(F32), hal[s, 3, :, at(k)]], axis=0)
                hm_s[s, :, at(k)] = hm
                fx_s[s, :, at(k)] = hm * ub
                fy_s[s, :, at(k)] = hm * vb
                ab_s[s, :, at(k)] = 2.0 * (h - seen) - w
        return carry

    lax.fori_loop(0, states, before_stress, 0)

    wait_cf()
    loads[5].wait()
    coeffs = jnp.concatenate([cfg[b] for b in range(LINE)], axis=1)
    pot[...] = lax.dot_general(
        coeffs, bc[...], (((1,), (1,)), ((), ())), preferred_element_type=F32
    )
    turns = {}
    for step in range(nk + 1):
        if step < nk:
            q = pot[0:ring, at(step)]
            turns[step] = turned(q)
            px[:, at(step)] = -0.15 * row_diff(q)
        if step >= 1:
            py[:, at(step - 1)] = 0.15 * column_diff(turns, step - 1)
    gx[...] = jnp.zeros_like(gx)
    gy[...] = jnp.zeros_like(gy)

    def with_stress(s, carry):
        ft, dyf, at_, rows_of, hms = {}, {}, {}, {}, {}
        for step in range(nk + 2):
            if step < nk:
                k = step
                hm = hm_s[s, :, at(k)]
                ft[k] = turned(fx_s[s, :, at(k)] + hm * px[:, at(k)])
                dyf[k] = row_diff(fy_s[s, :, at(k)] + hm * py[:, at(k)])
            if 1 <= step <= nk:
                k = step - 1
                a = mk[:, at(k)] * (ab_s[s, :, at(k)] - 0.15 * (column_diff(ft, k) + dyf.pop(k)))
                at_[k] = turned(a)
                rows_of[k] = row_diff(a)
            if step >= 2:
                k = step - 2
                hm = hm_s[s, :, at(k)]
                gx[:, at(k)] += hm * column_diff(at_, k)
                gy[:, at(k)] += hm * rows_of.pop(k)
        return carry

    lax.fori_loop(0, states, with_stress, 0)

    turns = {}
    per = piece // LANES
    for step in range(nk + 1):
        if step < nk:
            turns[step] = turned(gy[:, at(step)])
        if step >= 1:
            k = step - 1
            value = 0.005625 * (row_diff(gx[:, at(k)]) - column_diff(turns, k))
            gs[k // per, :, at(k % per)] = value[0:rows]

    gr[e] = gs[e]
    exchange(es, e, ENS, lambda p: gs.at[p], lambda p: gr.at[p])()
    summed = ((gr[0] + gr[1]) + (gr[2] + gr[3])).astype(BF16)
    part = jnp.dot(summed, bc[pl.ds(pl.multiple_of(e * piece, piece), piece), :], preferred_element_type=F32)
    for b in range(LINE):
        ps[b] = part[:, b * LANES : (b + 1) * LANES]
    pr[j] = ps[j]
    exchange(line, j, LINE, lambda p: ps.at[p], lambda p: pr.at[p])()
    projected = jnp.concatenate(
        [((pr[0] + pr[1]) + (pr[2] + pr[3])), ((pr[4] + pr[5]) + (pr[6] + pr[7]))], axis=0
    ).astype(BF16)

    rows2 = ext[:, 0:rows, :].reshape(2 * rows, basis)
    g_s[...] = lax.dot_general(
        rows2, projected, (((0,), (0,)), ((), ())), preferred_element_type=F32
    ).reshape(g_s.shape)
    exchange(ys, y, YN, lambda p: g_s.at[:, :, p], lambda p: gyr.at[p])()
    total = g_s[:, :, y]
    for i, (p, _) in enumerate(ys):
        total = total + gyr[p]
    gy_s[...] = total
    exchange(zs, z, zn, lambda p: gy_s.at[:, p], lambda p: gzr.at[p])()
    total = gy_s[:, z]
    for p, _ in zs:
        total = total + gzr[p]

    per_row = total.shape[1]
    squares = total * total
    flat = squares.reshape(2 * per_row // 8, 8, LANES)
    square = flat[0]
    for i in range(1, 2 * per_row // 8):
        square = square + flat[i]
    for b in range(2):
        fs[b, 0:per_row] = total[b]
        fs[b, per_row : per_row + 8] = square
    fr[j] = fs[x]
    exchange(line, j, LINE, lambda p: fs.at[p // ENS], lambda p: fr.at[p])()
    square = fr[0, per_row : per_row + 8]
    for b in range(1, LINE):
        square = square + fr[b, per_row : per_row + 8]
    sys_[...] = square
    syr[y] = square
    exchange(ys, y, YN, lambda p: sys_, lambda p: syr.at[p])()
    square = (syr[0] + syr[1]) + (syr[2] + syr[3])
    szs[...] = square
    szr[z] = square
    exchange(zs, z, zn, lambda p: szs, lambda p: szr.at[p])()
    square = szr[0]
    for b in range(1, zn):
        square = square + szr[b]
    mean = jnp.sum(square, keepdims=True) / (basis * basis)
    root = jnp.sqrt(mean + EPSILON)
    gradient = jnp.concatenate([fr[b, 0:per_row] for b in range(LINE)], axis=1)
    out_ref[...] = ct[...] - gradient / root

    for c in sent:
        c.wait_send()


def on_device(checkpoints, section_index, targets, sea_mask, basis_rows, basis_cols, control):
    states, slots, fields, rows, cols = checkpoints.shape
    basis = basis_cols.shape[1]
    per_row = control.shape[0]
    count = lax.axis_size("space")
    zn = count // (2 * YN)
    ring = rows + 8
    n_sems = 1 + 2 + YN + 2 + zn + 1 + LINE + ENS + LINE + YN + zn + LINE + YN + zn
    any_ = pl.BlockSpec(memory_space=pl.ANY)
    vmem = pltpu.VMEM
    scratch = [
        vmem((states, slots, fields, rows, cols), BF16),
        vmem((states, rows, cols), BF16),
        vmem((rows, cols), jnp.int32),
        vmem((rows, basis), BF16),
        vmem((cols, basis), BF16),
        vmem((per_row, basis), F32),
        vmem((LINE, per_row, LANES), BF16),
        vmem((2, zn, YN, per_row, LANES), BF16),
        vmem((2, rows + 16, basis), BF16),
        vmem((2, 16, basis), BF16),
        vmem((2, states // 2 + 1, 16, cols), BF16),
        vmem((2, states // 2 + 1, 16, cols), BF16),
        vmem((states, 4, 8, cols), F32),
        vmem((ring, cols), F32),
        vmem((states, ring, cols), F32),
        vmem((states, ring, cols), F32),
        vmem((states, ring, cols), F32),
        vmem((states, ring, cols), F32),
        vmem((2, rows + 16, LANES), BF16),
        vmem((LINE, rows + 16, LANES), BF16),
        vmem((rows + 16, cols), F32),
        vmem((ring, cols), F32),
        vmem((ring, cols), F32),
        vmem((ring, cols), F32),
        vmem((ring, cols), F32),
        vmem((ENS, rows, cols // ENS), F32),
        vmem((ENS, rows, cols // ENS), F32),
        vmem((LINE, rows, LANES), F32),
        vmem((LINE, rows, LANES), F32),
        vmem((2, zn, YN, per_row, LANES), F32),
        vmem((YN, 2, zn, per_row, LANES), F32),
        vmem((2, zn, per_row, LANES), F32),
        vmem((zn, 2, per_row, LANES), F32),
        vmem((2, per_row + 8, LANES), F32),
        vmem((LINE, per_row + 8, LANES), F32),
        vmem((8, LANES), F32),
        vmem((YN, 8, LANES), F32),
        vmem((8, LANES), F32),
        vmem((zn, 8, LANES), F32),
        pltpu.SemaphoreType.DMA((6,)),
        pltpu.SemaphoreType.DMA((n_sems,)),
        pltpu.SemaphoreType.DMA((n_sems,)),
    ]
    return pl.pallas_call(
        functools.partial(kernel, zn),
        out_shape=jax.ShapeDtypeStruct(control.shape, F32),
        in_specs=[pl.BlockSpec(memory_space=pltpu.SMEM)] + [any_] * 6,
        out_specs=pl.BlockSpec(memory_space=pltpu.VMEM),
        scratch_shapes=scratch,
        compiler_params=pltpu.CompilerParams(
            collective_id=0, has_side_effects=True, vmem_limit_bytes=60 * 1024 * 1024
        ),
    )(section_index, checkpoints, targets, sea_mask, basis_rows, basis_cols, control)


def solution(mesh):
    return jax.shard_map(
        on_device,
        mesh=mesh,
        in_specs=(
            P("ens", None, None, "space", None),
            P("ens"),
            P("ens", "space", None),
            P("space", None),
            P("space", None),
            P(),
            P("space", None),
        ),
        out_specs=P("space", None),
        check_vma=False,
    )
```

time: 897 us -> 79.5 us (0.09)
  waiting for transfers between devices: 614 us -> 0 us
  blocking collectives: 170 us -> 0 us
  Pallas kernels: 0 us -> 77.9 us
  starting transfers between devices: 48 us -> 0 us
  other arithmetic: 24.5 us -> 0 us
  between operations: 14.4 us -> 0.01 us
  local copies, waits for them, and re-layouts: 13.9 us -> 1.47 us
  matrix products: 10.1 us -> 0 us
    reduce_scatter x1 -> x0, waiting for transfers between devices: 315 us -> none  [on_device(): lax.psum_scatter(lax.dot_general(basis_rows, projected, (((0,), (0,)), ((...]
    all_gather x1 -> x0, waiting for transfers between devices: 274 us -> none  [on_device(): lax.all_gather(narrow, 'space', axis=0, tiled=True)]
    psum x2 -> x0, blocking collectives: 170 us -> none  [the longest x1 154 us: normalized(): total = lax.psum(jnp.sum(gradient_rows * gradient_rows), 'space')]
    pallas_call x0 -> x1, Pallas kernels: none -> 77.9 us  [on_device(): pl.pallas_call(functools.partial(kernel, zn), out_shape=jax.ShapeDtypeStr...]
    ppermute x10 -> x0, starting transfers between devices: 47.9 us -> none  [the longest x5 34.3 us: with_halo(): after = lax.ppermute(initial, axis, down)]
    ppermute x10 -> x0, waiting for transfers between devices: 24.1 us -> none  [the longest x5 21.1 us: with_halo(): before = lax.ppermute(last, axis, up)]
    mul x7 -> x0, other arithmetic: 10.8 us -> none  [the longest x2 6.82 us: height_change(): return -(across_columns((DEPTH + height) * east) + across_rows(flux_ext))]
    unnamed x19 -> x1, local copies, waits for them, and re-layouts: 11.8 us -> 1.47 us
  transfers between devices with their start and end apart: 12 -> 0, of which waited for: 9 -> 0; matrix products, arithmetic and copies ran while one was open for 2% -> 0% of each run, Pallas kernels for 0% -> 0%
where the time goes in v1:
time: 79.5 us; the launch traced here: 79.4 us
  Pallas kernels  77.9 us (98%)
  local copies, waits for them, and re-layouts  1.47 us (2%)
    pallas_call x1, Pallas kernels, on_device(): pl.pallas_call(functools.partial(kernel, zn), out_shape=jax.ShapeDtypeStr...  77.9 us

profile of v1, /device:TPU:2, one launch (start us, length us, event | category | flops | bytes accessed | tf_op | source)
XLA Modules:
  0.0 79.4 jit_solution(12375819337799871280)
XLA Ops:
  0.0 77.9 %shard_map.73 = f32[16,1024]{1,0:T(8,128)} custom-call(s32[8]{0:T(128)} %si_ref.1, bf16[8,2,3,32,2048]{4,3,2,1,0:T(8,128)(2,1)} %ck_hbm.1, bf16[8,32,2048]{2,1,0:T(8,128)(2,1)} %tg_hbm.1, s32[32,2048]{1,0:T(8,128)} %mask_hbm.1, bf16[32,1024]{1,0:T(8,128)(2,1)} %br_hbm.1, bf16[2048,1024]{1,0:T(8,128)(2,1)} %bc_hbm.1, f32[16,1024]{1,0:T(8,128)} %ct_hbm.1), custom_call_target="tpu_custom_call" | custom-call | tf_op jit(solution)/shard_map/pallas_call | solution.py:426
  77.9 1.5 %copy.9 = f32[16,1024]{1,0:T(8,128)} copy(f32[16,1024]{1,0:T(8,128)} %shard_map.73) | data formatting | bytes 131072

commit v2 on v1

--- a/solution.py
+++ b/solution.py
@@ -15,15 +15,16 @@
 LINE = 8
 ENS = 4
 YN = 4
+FOLD = 4
 
 
 def kernel(
     zn,
     si_ref, ck_hbm, tg_hbm, mask_hbm, br_hbm, bc_hbm, ct_hbm, out_ref,
-    ck, tg, mk_in, br, bc, ct,
-    ctl_s, ctl_g, ext, bhal, hs, hr, hal, mk,
+    ck, tg, mk_in, br, bc, ct, bcp, xin,
+    ctl_s, ctl_g, ext, bhal, hs, hr, mk, tmp,
     hm_s, fx_s, fy_s, ab_s, cfs, cfg, pot, px, py, gx, gy,
-    gs, gr, ps, pr, g_s, gyr, gy_s, gzr, fs, fr, sys_, syr, szs, szr,
+    gs, gr, ps, pr, g_s, gyr, gy_s, gzr, fs, fr, sls, slr, sys_, syr, szs, szr,
     load_sem, send_sem, recv_sem,
 ):
     states, rows, cols = ck.shape[0], ck.shape[3], ck.shape[4]
@@ -54,6 +55,10 @@
     for d in range(1, zn):
         z2 = (z + d) % zn
         zs.append((z2, dev(e, x, z2, y)))
+    xzs = []
+    for d in range(1, 2 * zn):
+        q2 = (x * zn + z + d) % (2 * zn)
+        xzs.append((q2, dev(e, q2 // zn, q2 % zn, y)))
     es = []
     for d in range(1, ENS):
         e2 = (e + d) % ENS
@@ -79,7 +84,7 @@
         load.start()
 
     barrier = pltpu.get_barrier_semaphore()
-    greet = [d for _, d in line] + [d for _, d in ys] + [d for _, d in zs] + [after, before]
+    greet = [d for _, d in xzs + line + ys] + [after, before]
     for d in greet:
         pl.semaphore_signal(barrier, inc=1, device_id=d, device_id_type=MESH)
 
@@ -119,13 +124,6 @@
     for b in range(LINE):
         ctl_s[b] = ct[:, b * LANES : (b + 1) * LANES].astype(BF16)
     ctl_g[x, z, y] = ctl_s[j]
-    pl.semaphore_wait(barrier, len(greet))
-    a0 = single(ctl_s.at[(1 - x) * ENS + e], ctl_g.at[x, z, y], partner)
-    loads[1].wait()
-    top_rows = single(br.at[0:16], bhal.at[0], before)
-    end_rows = single(br.at[rows - 16 : rows], bhal.at[1], after)
-    a0()
-    ay = exchange(ys, y, YN, lambda p: ctl_g.at[:, z, y], lambda p: ctl_g.at[:, z, p])
 
     loads[2].wait()
     loads[3].wait()
@@ -156,11 +154,46 @@
         down = jnp.where(sub == s, final if s == 7 else pltpu.roll(final, s + 1, 0), down)
     hs[0, states // 2] = jnp.concatenate([up, mk_in[0:8, :].astype(F32)], axis=0).astype(BF16)
     hs[1, states // 2] = jnp.concatenate([down, mk_in[rows - 8 : rows, :].astype(F32)], axis=0).astype(BF16)
+    loads[1].wait()
+
+    pl.semaphore_wait(barrier, len(greet))
+    axz = exchange(
+        xzs, x * zn + z, 2 * zn,
+        lambda p: ctl_s.at[(p // zn) * ENS + e],
+        lambda p: ctl_g.at[p // zn, p % zn, y],
+    )
+    top_rows = single(br.at[0:16], bhal.at[0], before)
+    end_rows = single(br.at[rows - 16 : rows], bhal.at[1], after)
     from_after = single(hs.at[0], hr.at[0], before)
     from_before = single(hs.at[1], hr.at[1], after)
 
-    ay()
-    az = exchange(zs, z, zn, lambda p: ctl_g.at[:, z], lambda p: ctl_g.at[:, p])
+    wide = FOLD * LANES
+    groups = cols // wide
+    source = lax.broadcasted_iota(jnp.int32, (wide, wide), 0)
+    place = lax.broadcasted_iota(jnp.int32, (wide, wide), 1)
+    fold = (source == FOLD * (place % LANES) + place // LANES).astype(F32).astype(BF16)
+
+    def folded(blocks):
+        lhs = jnp.concatenate([b[:, g * wide : (g + 1) * wide] for g in range(groups) for b in blocks], axis=0)
+        res = jnp.dot(lhs, fold, preferred_element_type=F32)
+        high = blocks[0].shape[0]
+        n = len(blocks)
+        return [
+            [res[(g * n + i) * high : (g * n + i + 1) * high] for g in range(groups)] for i in range(n)
+        ]
+
+    def own_rows(s, carry):
+        slot = si_ref[s]
+        parts = folded([ck[s, slot, 0], ck[s, slot, 1], ck[s, slot, 2], tg[s]])
+        for i in range(4):
+            for g in range(groups):
+                xin[s, i, 0:rows, g * wide : (g + 1) * wide] = parts[i][g]
+        return carry
+
+    lax.fori_loop(0, states, own_rows, 0)
+    (parts,) = folded([mk_in[...].astype(F32).astype(BF16)])
+    for g in range(groups):
+        mk[0:rows, g * wide : (g + 1) * wide] = parts[g]
 
     low_end = jnp.where(t < count - 1, 4, 0)
     high_start = jnp.where(t > 0, 4, 8)
@@ -177,33 +210,48 @@
     ext[x, rows : rows + 16] = jnp.concatenate([edge, jnp.zeros_like(edge)], axis=0).astype(BF16)
     other_ext = single(ext.at[x], ext.at[x], partner)
 
+    axz()
+    ay = exchange(ys, y, YN, lambda p: ctl_g.at[:, :, y], lambda p: ctl_g.at[:, :, p])
+
+    loads[5].wait()
+    fold_t = (place == FOLD * (source % LANES) + source // LANES).astype(F32).astype(BF16)
+
+    def basis_group(g, carry):
+        at_g = pl.ds(pl.multiple_of(g * wide, wide), wide)
+        bcp[at_g, :] = jnp.dot(fold_t, bc[at_g, :], preferred_element_type=F32).astype(BF16)
+        return carry
+
+    lax.fori_loop(0, groups, basis_group, 0)
+
     from_after()
     from_before()
+    subw = lax.broadcasted_iota(jnp.int32, (8, wide), 0)
 
     def joined(low, high):
-        return jnp.where(sub < low_end, low, jnp.where(sub >= high_start, high, 0.0))
-
-    for half in range(states // 2):
-        low2 = hr[0, half].astype(F32)
-        high2 = hr[1, half].astype(F32)
-        for i in range(2):
-            s = 2 * half + i
-            low, high = low2[8 * i : 8 * i + 8], high2[8 * i : 8 * i + 8]
-            hal[s, 0] = joined(low, high)
-            hal[s, 1] = joined(pltpu.roll(low, 2, 0), pltpu.roll(high, 6, 0))
-            hal[s, 2] = joined(pltpu.roll(low, 5, 0), pltpu.roll(high, 3, 0))
-    low2 = hr[0, states // 2].astype(F32)
-    high2 = hr[1, states // 2].astype(F32)
-    for s in range(states):
-        low, high = low2[0:8], high2[0:8]
-        low = low if s == 0 else pltpu.roll(low, 8 - s, 0)
-        high = high if s == 7 else pltpu.roll(high, 7 - s, 0)
-        hal[s, 3] = joined(low, high)
-    mk[0:rows] = mk_in[...].astype(F32)
-    mk[rows:ring] = joined(low2[8:16], high2[8:16])
-
-    az()
+        return jnp.where(subw < low_end, low, jnp.where(subw >= high_start, high, 0.0))
+
+    for half in range(states // 2 + 1):
+        low4, high4 = folded([hr[0, half], hr[1, half]])
+        for g in range(groups):
+            at_g = slice(g * wide, (g + 1) * wide)
+            low2, high2 = low4[g], high4[g]
+            if half < states // 2:
+                for i in range(2):
+                    s = 2 * half + i
+                    low, high = low2[8 * i : 8 * i + 8], high2[8 * i : 8 * i + 8]
+                    xin[s, 0, rows:ring, at_g] = joined(low, high)
+                    xin[s, 1, rows:ring, at_g] = joined(pltpu.roll(low, 2, 0), pltpu.roll(high, 6, 0))
+                    xin[s, 2, rows:ring, at_g] = joined(pltpu.roll(low, 5, 0), pltpu.roll(high, 3, 0))
+            else:
+                for s in range(states):
+                    low, high = low2[0:8], high2[0:8]
+                    low = low if s == 0 else pltpu.roll(low, 8 - s, 0)
+                    high = high if s == 7 else pltpu.roll(high, 7 - s, 0)
+                    xin[s, 3, rows:ring, at_g] = joined(low, high)
+                mk[rows:ring, at_g] = joined(low2[8:16], high2[8:16])
+
     other_ext()
+    ay()
     control_all = ctl_g[...].reshape(basis, LANES)
     lhs = ext[...].reshape(2 * (rows + 16), basis)
     cf = jnp.dot(lhs, control_all, preferred_element_type=F32).astype(BF16)
@@ -218,102 +266,99 @@
     def row_diff(q):
         return pltpu.roll(q, ring - 1, 0) - pltpu.roll(q, 1, 0)
 
-    def turned(q):
-        return pltpu.roll(q, LANES - 1, 1), pltpu.roll(q, 1, 1)
-
-    def column_diff(turns, k):
-        left = turns[k - 1][1] if k > 0 else 0.0
-        right = turns[k + 1][0] if k < nk - 1 else 0.0
-        return jnp.where(is_last, right, turns[k][0]) - jnp.where(is_first, left, turns[k][1])
+    def column_diff(get, k, turned):
+        g, p = divmod(k, FOLD)
+
+        def left(c):
+            if c not in turned:
+                turned[c] = pltpu.roll(get(c), LANES - 1, 1)
+            return turned[c]
+
+        def right(c):
+            if c not in turned:
+                turned[c] = pltpu.roll(get(c), 1, 1)
+            return turned[c]
+
+        if p < FOLD - 1:
+            plus = get(k + 1)
+        else:
+            plus = jnp.where(is_last, left(k + 1) if g < groups - 1 else 0.0, left(k - p))
+        if p > 0:
+            minus = get(k - 1)
+        else:
+            minus = jnp.where(is_first, right(k - 1) if g > 0 else 0.0, right(k + FOLD - 1))
+        return plus - minus
 
     def at(k):
         return slice(k * LANES, (k + 1) * LANES)
 
+    def chunks(g):
+        return range(g * FOLD, (g + 1) * FOLD)
+
     def before_stress(s, carry):
-        slot = si_ref[s]
-
-        def full(field, k):
-            own = ck[s, slot, field, :, at(k)].astype(F32)
-            return jnp.concatenate([own, hal[s, field, :, at(k)]], axis=0)
-
-        kept, fxt, ht = {}, {}, {}
-        for step in range(nk + 1):
-            if step < nk:
-                k = step
-                h, u, v = (full(f, k) for f in range(3))
-                g = 1.0 + h
-                fx, fy = g * u, g * v
-                kept[k] = (h, u, v, row_diff(fy), row_diff(h))
-                fxt[k], ht[k] = turned(fx), turned(h)
+        fxt, ht = {}, {}
+        for step in range(groups + 1):
+            if step < groups:
+                for k in chunks(step):
+                    tmp[0, :, at(k)] = (1.0 + xin[s, 0, :, at(k)]) * xin[s, 1, :, at(k)]
             if step >= 1:
-                k = step - 1
-                h, u, v, dyf, dyh = kept.pop(k)
-                w = 0.15 * (column_diff(fxt, k) + dyf)
-                hm = mk[:, at(k)] * ((1.0 + h) - w)
-                ub = 0.97 * u + 0.15 * (v - column_diff(ht, k))
-                vb = 0.97 * v - 0.15 * (u + dyh)
-                seen = jnp.concatenate([tg[s, :, at(k)].astype(F32), hal[s, 3, :, at(k)]], axis=0)
-                hm_s[s, :, at(k)] = hm
-                fx_s[s, :, at(k)] = hm * ub
-                fy_s[s, :, at(k)] = hm * vb
-                ab_s[s, :, at(k)] = 2.0 * (h - seen) - w
+                for k in chunks(step - 1):
+                    h, u, v, seen = (xin[s, f, :, at(k)] for f in range(4))
+                    g = 1.0 + h
+                    w = 0.15 * (column_diff(lambda c: tmp[0, :, at(c)], k, fxt) + row_diff(g * v))
+                    hm = mk[:, at(k)] * (g - w)
+                    dxh = column_diff(lambda c: xin[s, 0, :, at(c)], k, ht)
+                    hm_s[s, :, at(k)] = hm
+                    fx_s[s, :, at(k)] = hm * (0.97 * u + 0.15 * (v - dxh))
+                    fy_s[s, :, at(k)] = hm * (0.97 * v - 0.15 * (u + row_diff(h)))
+                    ab_s[s, :, at(k)] = 2.0 * (h - seen) - w
         return carry
 
     lax.fori_loop(0, states, before_stress, 0)
 
     wait_cf()
-    loads[5].wait()
     coeffs = jnp.concatenate([cfg[b] for b in range(LINE)], axis=1)
     pot[...] = lax.dot_general(
-        coeffs, bc[...], (((1,), (1,)), ((), ())), preferred_element_type=F32
+        coeffs, bcp[...], (((1,), (1,)), ((), ())), preferred_element_type=F32
     )
     turns = {}
-    for step in range(nk + 1):
-        if step < nk:
-            q = pot[0:ring, at(step)]
-            turns[step] = turned(q)
-            px[:, at(step)] = -0.15 * row_diff(q)
-        if step >= 1:
-            py[:, at(step - 1)] = 0.15 * column_diff(turns, step - 1)
+    for k in range(nk):
+        px[:, at(k)] = -0.15 * row_diff(pot[0:ring, at(k)])
+        py[:, at(k)] = 0.15 * column_diff(lambda c: pot[0:ring, at(c)], k, turns)
     gx[...] = jnp.zeros_like(gx)
     gy[...] = jnp.zeros_like(gy)
 
     def with_stress(s, carry):
-        ft, dyf, at_, rows_of, hms = {}, {}, {}, {}, {}
-        for step in range(nk + 2):
-            if step < nk:
-                k = step
-                hm = hm_s[s, :, at(k)]
-                ft[k] = turned(fx_s[s, :, at(k)] + hm * px[:, at(k)])
-                dyf[k] = row_diff(fy_s[s, :, at(k)] + hm * py[:, at(k)])
-            if 1 <= step <= nk:
-                k = step - 1
-                a = mk[:, at(k)] * (ab_s[s, :, at(k)] - 0.15 * (column_diff(ft, k) + dyf.pop(k)))
-                at_[k] = turned(a)
-                rows_of[k] = row_diff(a)
+        ft, at_ = {}, {}
+        for step in range(groups + 2):
+            if step < groups:
+                for k in chunks(step):
+                    tmp[0, :, at(k)] = fx_s[s, :, at(k)] + hm_s[s, :, at(k)] * px[:, at(k)]
+            if 1 <= step <= groups:
+                for k in chunks(step - 1):
+                    dyf = row_diff(fy_s[s, :, at(k)] + hm_s[s, :, at(k)] * py[:, at(k)])
+                    dxf = column_diff(lambda c: tmp[0, :, at(c)], k, ft)
+                    tmp[1, :, at(k)] = mk[:, at(k)] * (ab_s[s, :, at(k)] - 0.15 * (dxf + dyf))
             if step >= 2:
-                k = step - 2
-                hm = hm_s[s, :, at(k)]
-                gx[:, at(k)] += hm * column_diff(at_, k)
-                gy[:, at(k)] += hm * rows_of.pop(k)
+                for k in chunks(step - 2):
+                    hm = hm_s[s, :, at(k)]
+                    gx[:, at(k)] += hm * column_diff(lambda c: tmp[1, :, at(c)], k, at_)
+                    gy[:, at(k)] += hm * row_diff(tmp[1, :, at(k)])
         return carry
 
     lax.fori_loop(0, states, with_stress, 0)
 
     turns = {}
     per = piece // LANES
-    for step in range(nk + 1):
-        if step < nk:
-            turns[step] = turned(gy[:, at(step)])
-        if step >= 1:
-            k = step - 1
-            value = 0.005625 * (row_diff(gx[:, at(k)]) - column_diff(turns, k))
-            gs[k // per, :, at(k % per)] = value[0:rows]
+    for k in range(nk):
+        dyg = column_diff(lambda c: gy[:, at(c)], k, turns)
+        value = 0.005625 * (row_diff(gx[:, at(k)]) - dyg)
+        gs[k // per, :, at(k % per)] = value[0:rows]
 
     gr[e] = gs[e]
     exchange(es, e, ENS, lambda p: gs.at[p], lambda p: gr.at[p])()
     summed = ((gr[0] + gr[1]) + (gr[2] + gr[3])).astype(BF16)
-    part = jnp.dot(summed, bc[pl.ds(pl.multiple_of(e * piece, piece), piece), :], preferred_element_type=F32)
+    part = jnp.dot(summed, bcp[pl.ds(pl.multiple_of(e * piece, piece), piece), :], preferred_element_type=F32)
     for b in range(LINE):
         ps[b] = part[:, b * LANES : (b + 1) * LANES]
     pr[j] = ps[j]
@@ -326,14 +371,35 @@
     g_s[...] = lax.dot_general(
         rows2, projected, (((0,), (0,)), ((), ())), preferred_element_type=F32
     ).reshape(g_s.shape)
-    exchange(ys, y, YN, lambda p: g_s.at[:, :, p], lambda p: gyr.at[p])()
-    total = g_s[:, :, y]
-    for i, (p, _) in enumerate(ys):
-        total = total + gyr[p]
-    gy_s[...] = total
-    exchange(zs, z, zn, lambda p: gy_s.at[:, p], lambda p: gzr.at[p])()
-    total = gy_s[:, z]
-    for p, _ in zs:
+    order = [zn // 2]
+    for d in range(zn // 2 - 1, 0, -1):
+        order += [zn // 2 - (zn // 2 - d), zn - d]
+    order.append(0)
+    arrivals = {}
+    for off in order:
+        z2 = (z + off) % zn
+        arrivals[off] = exchange(
+            ys, y, YN,
+            lambda p, z2=z2: g_s.at[:, z2, p],
+            lambda p, off=off: gyr.at[off, p],
+        )
+    at_z = sems(zn)
+    for i, off in enumerate(order):
+        z2 = (z + off) % zn
+        arrivals[off]()
+        gyr[off, y] = g_s[:, z2, y]
+        total = (gyr[off, 0] + gyr[off, 1]) + (gyr[off, 2] + gyr[off, 3])
+        if off:
+            gy_s[off] = total
+            c = copy(gy_s.at[off], gzr.at[z], at_z + i, at_z + z, dev(e, x, z2, y))
+            c.start()
+            sent.append(c)
+        else:
+            gzr[z] = total
+    for p, device in zs:
+        copy(gy_s.at[0], gzr.at[p], at_z, at_z + p, device).wait_recv()
+    total = gzr[0]
+    for p in range(1, zn):
         total = total + gzr[p]
 
     per_row = total.shape[1]
@@ -342,14 +408,16 @@
     square = flat[0]
     for i in range(1, 2 * per_row // 8):
         square = square + flat[i]
-    for b in range(2):
-        fs[b, 0:per_row] = total[b]
-        fs[b, per_row : per_row + 8] = square
+    sls[...] = square
+    slr[j] = square
+    line_squares = exchange(line, j, LINE, lambda p: sls, lambda p: slr.at[p])
+    fs[...] = total
     fr[j] = fs[x]
-    exchange(line, j, LINE, lambda p: fs.at[p // ENS], lambda p: fr.at[p])()
-    square = fr[0, per_row : per_row + 8]
+    line_rows = exchange(line, j, LINE, lambda p: fs.at[p // ENS], lambda p: fr.at[p])
+    line_squares()
+    square = slr[0]
     for b in range(1, LINE):
-        square = square + fr[b, per_row : per_row + 8]
+        square = square + slr[b]
     sys_[...] = square
     syr[y] = square
     exchange(ys, y, YN, lambda p: sys_, lambda p: syr.at[p])()
@@ -362,7 +430,8 @@
         square = square + szr[b]
     mean = jnp.sum(square, keepdims=True) / (basis * basis)
     root = jnp.sqrt(mean + EPSILON)
-    gradient = jnp.concatenate([fr[b, 0:per_row] for b in range(LINE)], axis=1)
+    line_rows()
+    gradient = jnp.concatenate([fr[b] for b in range(LINE)], axis=1)
     out_ref[...] = ct[...] - gradient / root
 
     for c in sent:
@@ -376,7 +445,7 @@
     count = lax.axis_size("space")
     zn = count // (2 * YN)
     ring = rows + 8
-    n_sems = 1 + 2 + YN + 2 + zn + 1 + LINE + ENS + LINE + YN + zn + LINE + YN + zn
+    n_sems = 2 * zn + 4 + 1 + YN + LINE + ENS + LINE + zn * YN + zn + 2 * LINE + YN + zn
     any_ = pl.BlockSpec(memory_space=pl.ANY)
     vmem = pltpu.VMEM
     scratch = [
@@ -386,14 +455,16 @@
         vmem((rows, basis), BF16),
         vmem((cols, basis), BF16),
         vmem((per_row, basis), F32),
+        vmem((cols, basis), BF16),
+        vmem((states, 4, ring, cols), F32),
         vmem((LINE, per_row, LANES), BF16),
         vmem((2, zn, YN, per_row, LANES), BF16),
         vmem((2, rows + 16, basis), BF16),
         vmem((2, 16, basis), BF16),
         vmem((2, states // 2 + 1, 16, cols), BF16),
         vmem((2, states // 2 + 1, 16, cols), BF16),
-        vmem((states, 4, 8, cols), F32),
         vmem((ring, cols), F32),
+        vmem((2, ring, cols), F32),
         vmem((states, ring, cols), F32),
         vmem((states, ring, cols), F32),
         vmem((states, ring, cols), F32),
@@ -410,11 +481,13 @@
         vmem((LINE, rows, LANES), F32),
         vmem((LINE, rows, LANES), F32),
         vmem((2, zn, YN, per_row, LANES), F32),
-        vmem((YN, 2, zn, per_row, LANES), F32),
-        vmem((2, zn, per_row, LANES), F32),
+        vmem((zn, YN, 2, per_row, LANES), F32),
         vmem((zn, 2, per_row, LANES), F32),
-        vmem((2, per_row + 8, LANES), F32),
-        vmem((LINE, per_row + 8, LANES), F32),
+        vmem((zn, 2, per_row, LANES), F32),
+        vmem((2, per_row, LANES), F32),
+        vmem((LINE, per_row, LANES), F32),
+        vmem((8, LANES), F32),
+        vmem((LINE, 8, LANES), F32),
         vmem((8, LANES), F32),
         vmem((YN, 8, LANES), F32),
         vmem((8, LANES), F32),

time: 79.5 us -> 69.9 us (0.88)
  Pallas kernels: 77.9 us -> 68.2 us
    pallas_call x1, Pallas kernels: 77.9 us -> 68.2 us  [on_device(): pl.pallas_call(functools.partial(kernel, zn), out_shape=jax.ShapeDtypeStr...]
where the time goes in v2:
time: 69.9 us; the launch traced here: 69.6 us
  Pallas kernels  68.2 us (98%)
  local copies, waits for them, and re-layouts  1.47 us (2%)
    pallas_call x1, Pallas kernels, on_device(): pl.pallas_call(functools.partial(kernel, zn), out_shape=jax.ShapeDtypeStr...  68.2 us
    unnamed x1, local copies, waits for them, and re-layouts  1.47 us

profile of v2, /device:TPU:2, one launch (start us, length us, event | category | flops | bytes accessed | tf_op | source)
XLA Modules:
  0.0 69.6 jit_solution(16914730394302001682)
XLA Ops:
  0.0 68.2 %shard_map.73 = f32[16,1024]{1,0:T(8,128)} custom-call(s32[8]{0:T(128)} %si_ref.1, bf16[8,2,3,32,2048]{4,3,2,1,0:T(8,128)(2,1)} %ck_hbm.1, bf16[8,32,2048]{2,1,0:T(8,128)(2,1)} %tg_hbm.1, s32[32,2048]{1,0:T(8,128)} %mask_hbm.1, bf16[32,1024]{1,0:T(8,128)(2,1)} %br_hbm.1, bf16[2048,1024]{1,0:T(8,128)(2,1)} %bc_hbm.1, f32[16,1024]{1,0:T(8,128)} %ct_hbm.1), custom_call_target="tpu_custom_call" | custom-call | tf_op jit(solution)/shard_map/pallas_call | solution.py:499
  68.2 1.5 %copy.9 = f32[16,1024]{1,0:T(8,128)} copy(f32[16,1024]{1,0:T(8,128)} %shard_map.73) | data formatting | bytes 131072

commit v3 on v2

--- a/solution.py
+++ b/solution.py
@@ -15,6 +15,7 @@
 LINE = 8
 ENS = 4
 YN = 4
+EARLY = 2
 FOLD = 4
 
 
@@ -24,7 +25,7 @@
     ck, tg, mk_in, br, bc, ct, bcp, xin,
     ctl_s, ctl_g, ext, bhal, hs, hr, mk, tmp,
     hm_s, fx_s, fy_s, ab_s, cfs, cfg, pot, px, py, gx, gy,
-    gs, gr, ps, pr, g_s, gyr, gy_s, gzr, fs, fr, sls, slr, sys_, syr, szs, szr,
+    gs, gr, ps, pr, g_s, g_n, gyr, gy_s, gzr, fs, fr, sls, slr, sys_, syr, szs, szr,
     load_sem, send_sem, recv_sem,
 ):
     states, rows, cols = ck.shape[0], ck.shape[3], ck.shape[4]
@@ -74,14 +75,13 @@
         base[0] += n
         return at
 
-    loads = [
-        pltpu.make_async_copy(src, dst, load_sem.at[i])
-        for i, (src, dst) in enumerate(
-            ((ct_hbm, ct), (br_hbm, br), (ck_hbm, ck), (tg_hbm, tg), (mask_hbm, mk_in), (bc_hbm, bc))
-        )
-    ]
+    moves = [(ct_hbm, ct), (br_hbm, br)]
+    moves += [(ck_hbm.at[i], ck.at[i]) for i in range(states)]
+    moves += [(tg_hbm, tg), (mask_hbm, mk_in), (bc_hbm, bc)]
+    loads = [pltpu.make_async_copy(src, dst, load_sem.at[i]) for i, (src, dst) in enumerate(moves)]
     for load in loads:
         load.start()
+    n_ck = 2
 
     barrier = pltpu.get_barrier_semaphore()
     greet = [d for _, d in xzs + line + ys] + [after, before]
@@ -125,26 +125,44 @@
         ctl_s[b] = ct[:, b * LANES : (b + 1) * LANES].astype(BF16)
     ctl_g[x, z, y] = ctl_s[j]
 
-    loads[2].wait()
-    loads[3].wait()
-    loads[4].wait()
+    pl.semaphore_wait(barrier, len(greet))
+    axz = exchange(
+        xzs, x * zn + z, 2 * zn,
+        lambda p: ctl_s.at[(p // zn) * ENS + e],
+        lambda p: ctl_g.at[p // zn, p % zn, y],
+    )
+    loads[1].wait()
+    top_rows = single(br.at[0:16], bhal.at[0], before)
+    end_rows = single(br.at[rows - 16 : rows], bhal.at[1], after)
+
     sub = lax.broadcasted_iota(jnp.int32, (8, cols), 0)
 
     def tiles(s, field, first):
-        slot = si_ref[s]
-        block = ck[s, slot, field, first : first + 16, :].astype(F32)
+        at_rows = slice(first, first + 16)
+        block = jnp.where(
+            si_ref[s] == 0, ck[s, 0, field, at_rows, :].astype(F32), ck[s, 1, field, at_rows, :].astype(F32)
+        )
         return block[0:8] if first == 0 else block[8:16]
 
     last = rows - 16
+    edges = []
     for half in range(states // 2):
+        if half == EARLY:
+            axz()
+            ay = exchange(ys, y, YN, lambda p: ctl_g.at[:, :, y], lambda p: ctl_g.at[:, :, p])
         up, down = [], []
         for s in (2 * half, 2 * half + 1):
+            loads[n_ck + s].wait()
             h, u, v = (tiles(s, f, 0) for f in range(3))
             up.append(jnp.where(sub < 3, h, jnp.where(sub < 6, pltpu.roll(v, 3, 0), pltpu.roll(u, 6, 0))))
             h, u, v = (tiles(s, f, last) for f in range(3))
             down.append(jnp.where(sub >= 5, h, jnp.where(sub >= 2, pltpu.roll(v, 5, 0), pltpu.roll(u, 2, 0))))
         hs[0, half] = jnp.concatenate(up, axis=0).astype(BF16)
         hs[1, half] = jnp.concatenate(down, axis=0).astype(BF16)
+        edges.append(single(hs.at[0, half], hr.at[0, half], before))
+        edges.append(single(hs.at[1, half], hr.at[1, half], after))
+    loads[n_ck + states].wait()
+    loads[n_ck + states + 1].wait()
     up = jnp.zeros((8, cols), F32)
     down = jnp.zeros((8, cols), F32)
     for s in range(states):
@@ -152,20 +170,11 @@
         up = jnp.where(sub == s, first if s == 0 else pltpu.roll(first, s, 0), up)
         final = tg[s, last : last + 16, :].astype(F32)[8:16]
         down = jnp.where(sub == s, final if s == 7 else pltpu.roll(final, s + 1, 0), down)
-    hs[0, states // 2] = jnp.concatenate([up, mk_in[0:8, :].astype(F32)], axis=0).astype(BF16)
-    hs[1, states // 2] = jnp.concatenate([down, mk_in[rows - 8 : rows, :].astype(F32)], axis=0).astype(BF16)
-    loads[1].wait()
-
-    pl.semaphore_wait(barrier, len(greet))
-    axz = exchange(
-        xzs, x * zn + z, 2 * zn,
-        lambda p: ctl_s.at[(p // zn) * ENS + e],
-        lambda p: ctl_g.at[p // zn, p % zn, y],
-    )
-    top_rows = single(br.at[0:16], bhal.at[0], before)
-    end_rows = single(br.at[rows - 16 : rows], bhal.at[1], after)
-    from_after = single(hs.at[0], hr.at[0], before)
-    from_before = single(hs.at[1], hr.at[1], after)
+    half = states // 2
+    hs[0, half] = jnp.concatenate([up, mk_in[0:8, :].astype(F32)], axis=0).astype(BF16)
+    hs[1, half] = jnp.concatenate([down, mk_in[rows - 8 : rows, :].astype(F32)], axis=0).astype(BF16)
+    edges.append(single(hs.at[0, half], hr.at[0, half], before))
+    edges.append(single(hs.at[1, half], hr.at[1, half], after))
 
     wide = FOLD * LANES
     groups = cols // wide
@@ -181,19 +190,6 @@
         return [
             [res[(g * n + i) * high : (g * n + i + 1) * high] for g in range(groups)] for i in range(n)
         ]
-
-    def own_rows(s, carry):
-        slot = si_ref[s]
-        parts = folded([ck[s, slot, 0], ck[s, slot, 1], ck[s, slot, 2], tg[s]])
-        for i in range(4):
-            for g in range(groups):
-                xin[s, i, 0:rows, g * wide : (g + 1) * wide] = parts[i][g]
-        return carry
-
-    lax.fori_loop(0, states, own_rows, 0)
-    (parts,) = folded([mk_in[...].astype(F32).astype(BF16)])
-    for g in range(groups):
-        mk[0:rows, g * wide : (g + 1) * wide] = parts[g]
 
     low_end = jnp.where(t < count - 1, 4, 0)
     high_start = jnp.where(t > 0, 4, 8)
@@ -210,10 +206,20 @@
     ext[x, rows : rows + 16] = jnp.concatenate([edge, jnp.zeros_like(edge)], axis=0).astype(BF16)
     other_ext = single(ext.at[x], ext.at[x], partner)
 
-    axz()
-    ay = exchange(ys, y, YN, lambda p: ctl_g.at[:, :, y], lambda p: ctl_g.at[:, :, p])
-
-    loads[5].wait()
+    def own_rows(s, carry):
+        slot = si_ref[s]
+        parts = folded([ck[s, slot, 0], ck[s, slot, 1], ck[s, slot, 2], tg[s]])
+        for i in range(4):
+            for g in range(groups):
+                xin[s, i, 0:rows, g * wide : (g + 1) * wide] = parts[i][g]
+        return carry
+
+    lax.fori_loop(0, states, own_rows, 0)
+    (parts,) = folded([mk_in[...].astype(F32).astype(BF16)])
+    for g in range(groups):
+        mk[0:rows, g * wide : (g + 1) * wide] = parts[g]
+
+    loads[n_ck + states + 2].wait()
     fold_t = (place == FOLD * (source % LANES) + source // LANES).astype(F32).astype(BF16)
 
     def basis_group(g, carry):
@@ -223,8 +229,17 @@
 
     lax.fori_loop(0, groups, basis_group, 0)
 
-    from_after()
-    from_before()
+    other_ext()
+    ay()
+    control_all = ctl_g[...].reshape(basis, LANES)
+    lhs = ext[...].reshape(2 * (rows + 16), basis)
+    cf = jnp.dot(lhs, control_all, preferred_element_type=F32).astype(BF16)
+    cfs[...] = cf.reshape(2, rows + 16, LANES)
+    cfg[j] = cfs[x]
+    wait_cf = exchange(line, j, LINE, lambda p: cfs.at[p // ENS], lambda p: cfg.at[p])
+
+    for wait_edge in edges:
+        wait_edge()
     subw = lax.broadcasted_iota(jnp.int32, (8, wide), 0)
 
     def joined(low, high):
@@ -250,15 +265,6 @@
                     xin[s, 3, rows:ring, at_g] = joined(low, high)
                 mk[rows:ring, at_g] = joined(low2[8:16], high2[8:16])
 
-    other_ext()
-    ay()
-    control_all = ctl_g[...].reshape(basis, LANES)
-    lhs = ext[...].reshape(2 * (rows + 16), basis)
-    cf = jnp.dot(lhs, control_all, preferred_element_type=F32).astype(BF16)
-    cfs[...] = cf.reshape(2, rows + 16, LANES)
-    cfg[j] = cfs[x]
-    wait_cf = exchange(line, j, LINE, lambda p: cfs.at[p // ENS], lambda p: cfg.at[p])
-
     lane = lax.broadcasted_iota(jnp.int32, (ring, LANES), 1)
     is_first = lane == 0
     is_last = lane == LANES - 1
@@ -371,6 +377,7 @@
     g_s[...] = lax.dot_general(
         rows2, projected, (((0,), (0,)), ((), ())), preferred_element_type=F32
     ).reshape(g_s.shape)
+    g_n[...] = g_s[...].astype(BF16)
     order = [zn // 2]
     for d in range(zn // 2 - 1, 0, -1):
         order += [zn // 2 - (zn // 2 - d), zn - d]
@@ -380,15 +387,16 @@
         z2 = (z + off) % zn
         arrivals[off] = exchange(
             ys, y, YN,
-            lambda p, z2=z2: g_s.at[:, z2, p],
+            lambda p, z2=z2: g_n.at[:, z2, p],
             lambda p, off=off: gyr.at[off, p],
         )
     at_z = sems(zn)
     for i, off in enumerate(order):
         z2 = (z + off) % zn
         arrivals[off]()
-        gyr[off, y] = g_s[:, z2, y]
-        total = (gyr[off, 0] + gyr[off, 1]) + (gyr[off, 2] + gyr[off, 3])
+        total = g_s[:, z2, y]
+        for p, _ in ys:
+            total = total + gyr[off, p].astype(F32)
         if off:
             gy_s[off] = total
             c = copy(gy_s.at[off], gzr.at[z], at_z + i, at_z + z, dev(e, x, z2, y))
@@ -445,7 +453,7 @@
     count = lax.axis_size("space")
     zn = count // (2 * YN)
     ring = rows + 8
-    n_sems = 2 * zn + 4 + 1 + YN + LINE + ENS + LINE + zn * YN + zn + 2 * LINE + YN + zn
+    n_sems = 2 * zn + 2 + 2 * (states // 2 + 1) + 1 + YN + LINE + ENS + LINE + zn * YN + zn + 2 * LINE + YN + zn
     any_ = pl.BlockSpec(memory_space=pl.ANY)
     vmem = pltpu.VMEM
     scratch = [
@@ -481,7 +489,8 @@
         vmem((LINE, rows, LANES), F32),
         vmem((LINE, rows, LANES), F32),
         vmem((2, zn, YN, per_row, LANES), F32),
-        vmem((zn, YN, 2, per_row, LANES), F32),
+        vmem((2, zn, YN, per_row, LANES), BF16),
+        vmem((zn, YN, 2, per_row, LANES), BF16),
         vmem((zn, 2, per_row, LANES), F32),
         vmem((zn, 2, per_row, LANES), F32),
         vmem((2, per_row, LANES), F32),
@@ -492,7 +501,7 @@
         vmem((YN, 8, LANES), F32),
         vmem((8, LANES), F32),
         vmem((zn, 8, LANES), F32),
-        pltpu.SemaphoreType.DMA((6,)),
+        pltpu.SemaphoreType.DMA((states + 5,)),
         pltpu.SemaphoreType.DMA((n_sems,)),
         pltpu.SemaphoreType.DMA((n_sems,)),
     ]

time: 69.9 us -> 68.3 us (0.977)
  Pallas kernels: 68.2 us -> 66.6 us
    pallas_call x1, Pallas kernels: 68.2 us -> 66.6 us  [on_device(): pl.pallas_call(functools.partial(kernel, zn), out_shape=jax.ShapeDtypeStr...]
where the time goes in v3:
time: 68.3 us; the launch traced here: 68.1 us
  Pallas kernels  66.6 us (98%)
  local copies, waits for them, and re-layouts  1.47 us (2%)
    pallas_call x1, Pallas kernels, on_device(): pl.pallas_call(functools.partial(kernel, zn), out_shape=jax.ShapeDtypeStr...  66.6 us
    unnamed x1, local copies, waits for them, and re-layouts  1.47 us

profile of v3, /device:TPU:2, one launch (start us, length us, event | category | flops | bytes accessed | tf_op | source)
XLA Modules:
  0.0 68.1 jit_solution(3348176060700511201)
XLA Ops:
  0.0 66.6 %shard_map.73 = f32[16,1024]{1,0:T(8,128)} custom-call(s32[8]{0:T(128)} %si_ref.1, bf16[8,2,3,32,2048]{4,3,2,1,0:T(8,128)(2,1)} %ck_hbm.1, bf16[8,32,2048]{2,1,0:T(8,128)(2,1)} %tg_hbm.1, s32[32,2048]{1,0:T(8,128)} %mask_hbm.1, bf16[32,1024]{1,0:T(8,128)(2,1)} %br_hbm.1, bf16[2048,1024]{1,0:T(8,128)(2,1)} %bc_hbm.1, f32[16,1024]{1,0:T(8,128)} %ct_hbm.1), custom_call_target="tpu_custom_call" | custom-call | tf_op jit(solution)/shard_map/pallas_call | solution.py:508
  66.6 1.5 %copy.9 = f32[16,1024]{1,0:T(8,128)} copy(f32[16,1024]{1,0:T(8,128)} %shard_map.73) | data formatting | bytes 131072

commit v4 on v3

--- a/solution.py
+++ b/solution.py
@@ -25,7 +25,7 @@
     ck, tg, mk_in, br, bc, ct, bcp, xin,
     ctl_s, ctl_g, ext, bhal, hs, hr, mk, tmp,
     hm_s, fx_s, fy_s, ab_s, cfs, cfg, pot, px, py, gx, gy,
-    gs, gr, ps, pr, g_s, g_n, gyr, gy_s, gzr, fs, fr, sls, slr, sys_, syr, szs, szr,
+    gs, gr, ps, pr, g_s, g_n, gfr, gyr, gy_s, gzr, fs, fr, sls, slr, sys_, syr, szs, szr,
     load_sem, send_sem, recv_sem,
 ):
     states, rows, cols = ck.shape[0], ck.shape[3], ck.shape[4]
@@ -377,7 +377,7 @@
     g_s[...] = lax.dot_general(
         rows2, projected, (((0,), (0,)), ((), ())), preferred_element_type=F32
     ).reshape(g_s.shape)
-    g_n[...] = g_s[...].astype(BF16)
+    g_n[...] = g_s[:, :, ys[1][0]].astype(BF16)
     order = [zn // 2]
     for d in range(zn // 2 - 1, 0, -1):
         order += [zn // 2 - (zn // 2 - d), zn - d]
@@ -385,18 +385,19 @@
     arrivals = {}
     for off in order:
         z2 = (z + off) % zn
-        arrivals[off] = exchange(
-            ys, y, YN,
-            lambda p, z2=z2: g_n.at[:, z2, p],
+        far = single(g_n.at[:, z2], gfr.at[off], ys[1][1])
+        near = exchange(
+            (ys[0], ys[2]), y, YN,
+            lambda p, z2=z2: g_s.at[:, z2, p],
             lambda p, off=off: gyr.at[off, p],
         )
+        arrivals[off] = (far, near)
     at_z = sems(zn)
     for i, off in enumerate(order):
         z2 = (z + off) % zn
-        arrivals[off]()
-        total = g_s[:, z2, y]
-        for p, _ in ys:
-            total = total + gyr[off, p].astype(F32)
+        for wait in arrivals[off]:
+            wait()
+        total = (gyr[off, ys[0][0]] + gyr[off, ys[2][0]]) + (g_s[:, z2, y] + gfr[off].astype(F32))
         if off:
             gy_s[off] = total
             c = copy(gy_s.at[off], gzr.at[z], at_z + i, at_z + z, dev(e, x, z2, y))
@@ -432,17 +433,21 @@
     square = (syr[0] + syr[1]) + (syr[2] + syr[3])
     szs[...] = square
     szr[z] = square
-    exchange(zs, z, zn, lambda p: szs, lambda p: szr.at[p])()
+    early = list(sent)
+    wait_squares = exchange(zs, z, zn, lambda p: szs, lambda p: szr.at[p])
+    line_rows()
+    gradient = jnp.concatenate([fr[b] for b in range(LINE)], axis=1)
+    for c in early:
+        c.wait_send()
+    wait_squares()
     square = szr[0]
     for b in range(1, zn):
         square = square + szr[b]
     mean = jnp.sum(square, keepdims=True) / (basis * basis)
     root = jnp.sqrt(mean + EPSILON)
-    line_rows()
-    gradient = jnp.concatenate([fr[b] for b in range(LINE)], axis=1)
     out_ref[...] = ct[...] - gradient / root
 
-    for c in sent:
+    for c in sent[len(early) :]:
         c.wait_send()
 
 
@@ -453,7 +458,7 @@
     count = lax.axis_size("space")
     zn = count // (2 * YN)
     ring = rows + 8
-    n_sems = 2 * zn + 2 + 2 * (states // 2 + 1) + 1 + YN + LINE + ENS + LINE + zn * YN + zn + 2 * LINE + YN + zn
+    n_sems = 2 * zn + 2 + 2 * (states // 2 + 1) + 1 + YN + LINE + ENS + LINE + zn * (YN + 1) + zn + 2 * LINE + YN + zn
     any_ = pl.BlockSpec(memory_space=pl.ANY)
     vmem = pltpu.VMEM
     scratch = [
@@ -489,8 +494,9 @@
         vmem((LINE, rows, LANES), F32),
         vmem((LINE, rows, LANES), F32),
         vmem((2, zn, YN, per_row, LANES), F32),
-        vmem((2, zn, YN, per_row, LANES), BF16),
-        vmem((zn, YN, 2, per_row, LANES), BF16),
+        vmem((2, zn, per_row, LANES), BF16),
+        vmem((zn, 2, per_row, LANES), BF16),
+        vmem((zn, YN, 2, per_row, LANES), F32),
         vmem((zn, 2, per_row, LANES), F32),
         vmem((zn, 2, per_row, LANES), F32),
         vmem((2, per_row, LANES), F32),

time: 68.3 us -> 68.3 us (level)
  no operation moved by 1% of the time
where the time goes in v4:
time: 68.3 us; the launch traced here: 68.1 us
  Pallas kernels  66.6 us (98%)
  local copies, waits for them, and re-layouts  1.47 us (2%)
    pallas_call x1, Pallas kernels, on_device(): pl.pallas_call(functools.partial(kernel, zn), out_shape=jax.ShapeDtypeStr...  66.6 us
    unnamed x1, local copies, waits for them, and re-layouts  1.47 us

profile of v4, /device:TPU:2, one launch (start us, length us, event | category | flops | bytes accessed | tf_op | source)
XLA Modules:
  0.0 68.1 jit_solution(7684356954452979092)
XLA Ops:
  0.0 66.6 %shard_map.73 = f32[16,1024]{1,0:T(8,128)} custom-call(s32[8]{0:T(128)} %si_ref.1, bf16[8,2,3,32,2048]{4,3,2,1,0:T(8,128)(2,1)} %ck_hbm.1, bf16[8,32,2048]{2,1,0:T(8,128)(2,1)} %tg_hbm.1, s32[32,2048]{1,0:T(8,128)} %mask_hbm.1, bf16[32,1024]{1,0:T(8,128)(2,1)} %br_hbm.1, bf16[2048,1024]{1,0:T(8,128)(2,1)} %bc_hbm.1, f32[16,1024]{1,0:T(8,128)} %ct_hbm.1), custom_call_target="tpu_custom_call" | custom-call | tf_op jit(solution)/shard_map/pallas_call | solution.py:514
  66.7 1.5 %copy.9 = f32[16,1024]{1,0:T(8,128)} copy(f32[16,1024]{1,0:T(8,128)} %shard_map.73) | data formatting | bytes 131072

commit v5 on v4

--- a/solution.py
+++ b/solution.py
@@ -356,13 +356,27 @@
 
     turns = {}
     per = piece // LANES
+    at_e = sems(ENS)
+
+    def to_ens(p, device):
+        return copy(gs.at[p], gr.at[e], at_e + p, at_e + e, device)
+
+    def quarter(p):
+        @pl.when(e != p)
+        def _():
+            to_ens(p, (p, t)).start()
+
     for k in range(nk):
         dyg = column_diff(lambda c: gy[:, at(c)], k, turns)
         value = 0.005625 * (row_diff(gx[:, at(k)]) - dyg)
         gs[k // per, :, at(k % per)] = value[0:rows]
+        if k % per == per - 1:
+            quarter(k // per)
 
     gr[e] = gs[e]
-    exchange(es, e, ENS, lambda p: gs.at[p], lambda p: gr.at[p])()
+    for p, device in es:
+        copy(gs.at[p], gr.at[p], at_e, at_e + p, device).wait_recv()
+        sent.append(to_ens(p, device))
     summed = ((gr[0] + gr[1]) + (gr[2] + gr[3])).astype(BF16)
     part = jnp.dot(summed, bcp[pl.ds(pl.multiple_of(e * piece, piece), piece), :], preferred_element_type=F32)
     for b in range(LINE):

time: 68.3 us -> 68.3 us (level)
  no operation moved by 1% of the time
where the time goes in v5:
time: 68.3 us; the launch traced here: 68.1 us
  Pallas kernels  66.6 us (98%)
  local copies, waits for them, and re-layouts  1.47 us (2%)
    pallas_call x1, Pallas kernels, on_device(): pl.pallas_call(functools.partial(kernel, zn), out_shape=jax.ShapeDtypeStr...  66.6 us
    unnamed x1, local copies, waits for them, and re-layouts  1.47 us

profile of v5, /device:TPU:2, one launch (start us, length us, event | category | flops | bytes accessed | tf_op | source)
XLA Modules:
  0.0 68.1 jit_solution(4842157907560971160)
XLA Ops:
  0.0 66.6 %shard_map.73 = f32[16,1024]{1,0:T(8,128)} custom-call(s32[8]{0:T(128)} %si_ref.1, bf16[8,2,3,32,2048]{4,3,2,1,0:T(8,128)(2,1)} %ck_hbm.1, bf16[8,32,2048]{2,1,0:T(8,128)(2,1)} %tg_hbm.1, s32[32,2048]{1,0:T(8,128)} %mask_hbm.1, bf16[32,1024]{1,0:T(8,128)(2,1)} %br_hbm.1, bf16[2048,1024]{1,0:T(8,128)(2,1)} %bc_hbm.1, f32[16,1024]{1,0:T(8,128)} %ct_hbm.1), custom_call_target="tpu_custom_call" | custom-call | tf_op jit(solution)/shard_map/pallas_call | solution.py:528
  66.6 1.5 %copy.9 = f32[16,1024]{1,0:T(8,128)} copy(f32[16,1024]{1,0:T(8,128)} %shard_map.73) | data formatting | bytes 131072
